TPU v7x, 128 devices: a whole 4x4x4 slice. The times are simulated.
128 devices in a mesh: row: 16 (over z, y_hi, core), col: 8 (over x, y_lo).
Axes of the slice: x: 4, y: 4 (y_hi: 2, y_lo: 2; y = y_hi * 2 + y_lo), z: 4, core: 2. Of those that a mesh axis runs over, the one named last changes fastest.
Arguments:
- features: bfloat16 [65536, 256], P(('row', 'col')), may hold values from -6 to 6
- tile_values: bfloat16 [16, 8, 512, 128, 128], P('row', 'col'), may hold values from 0 to 1, as said below
- tile_index: int32 [16, 8, 512], P('row', 'col'), may hold values from 0 to 2047, as said below
- tile_count: int32 [16, 8], P('row', 'col'), may hold values from 64 to 512
- weight: bfloat16 [256, 256], replicated, may hold values from -0.375 to 0.375
- out_bias: float32 [256], replicated, may hold values from -3 to 3
Outputs:
- layer_out: bfloat16 [65536, 256], P(('row', 'col'))
Inputs may be any that keep to these rules, and one draw needn't show every extreme that they name: `tile_index`: in each grid block the first tile_count entries name distinct tiles. `tile_values`: edge weights are bfloat16 values in [0, 1).
All inputs are finite; a program needn't handle non-finite values.
Results may differ from a plain program's by a relative error of at most 0.0047.
Values may be sent and summed in bfloat16 or wider, within the bound.
A program may use at most 128 MiB of HBM per device.

v0:
```python
import jax
import jax.numpy as jnp
from jax import lax
from jax.sharding import PartitionSpec as P


def accumulate(slot_values, positions, live_count, gathered, row_offset, row_span):
    slot_total = slot_values.shape[0]
    tile_size = slot_values.shape[1]
    feature_width = gathered.shape[1]
    col_tiles = gathered.shape[0] // tile_size
    sources_all = gathered.reshape(col_tiles, tile_size, feature_width)
    group_size = min(32, slot_total)
    turn_count = (live_count + group_size - 1) // group_size

    def one_turn(turn_id, carry):
        acc_total, acc_degree = carry
        turn_begin = (turn_id * group_size).astype(jnp.int32)
        first_slot = jnp.minimum(turn_begin, slot_total - group_size)
        tile_block = lax.dynamic_slice_in_dim(slot_values, first_slot, group_size, 0)
        slot_pos = lax.dynamic_slice_in_dim(positions, first_slot, group_size, 0)
        slot_ids = first_slot + jnp.arange(group_size, dtype=jnp.int32)
        tile_rows = slot_pos // col_tiles
        tile_cols = slot_pos % col_tiles
        in_range = (tile_rows >= row_offset) & (tile_rows < row_offset + row_span)
        live_mask = ((slot_ids >= turn_begin) & (slot_ids < live_count) & in_range).astype(
            jnp.float32
        )
        local_rows = jnp.clip(tile_rows, 0, row_span - 1)
        sources = sources_all[tile_cols]
        products = jnp.einsum(
            "gij,gjf->gif", tile_block, sources, preferred_element_type=jnp.float32
        )
        products = products * live_mask[:, None, None]
        acc_total = acc_total.at[local_rows].add(products)
        row_sums = jnp.sum(tile_block, axis=2, dtype=jnp.float32) * live_mask[:, None]
        return (acc_total, acc_degree.at[local_rows].add(row_sums))

    zero_total = jnp.zeros((row_span, tile_size, feature_width), jnp.float32)
    zero_degree = jnp.zeros((row_span, tile_size), jnp.float32)
    return lax.fori_loop(0, turn_count, one_turn, (zero_total, zero_degree))


def on_device(features, tile_values, tile_index, tile_count, weight, out_bias):
    slot_values = tile_values.reshape(tile_values.shape[2:])
    positions = tile_index.reshape(-1)
    live_count = tile_count.reshape(())
    tile_size = slot_values.shape[1]
    feature_width = features.shape[1]
    row_tiles = lax.axis_size("col") * features.shape[0] // tile_size
    gathered = lax.all_gather(features, "row", axis=0, tiled=True)
    part_total, part_degree = accumulate(
        slot_values, positions, live_count, gathered, jnp.int32(0), row_tiles
    )
    aggregate, degree = (
        lax.psum_scatter(
            part_total.reshape(-1, feature_width), "col", scatter_dimension=0, tiled=True
        ),
        lax.psum_scatter(part_degree.reshape(-1), "col", scatter_dimension=0, tiled=True),
    )
    hidden = (aggregate * lax.rsqrt(1.0 + degree)[:, None] + features.astype(jnp.float32)).astype(
        jnp.bfloat16
    )
    mixed = jnp.dot(hidden, weight, preferred_element_type=jnp.float32) + out_bias
    return jnp.maximum(mixed, 0.0).astype(jnp.bfloat16)


def solution(mesh):
    in_specs = (
        P(("row", "col"), None),
        P("row", "col", None, None, None),
        P("row", "col", None),
        P("row", "col"),
        P(),
        P(),
    )
    out_specs = P(("row", "col"), None)
    return jax.shard_map(
        on_device, mesh=mesh, in_specs=in_specs, out_specs=out_specs, check_vma=False
    )
```

profile of v0, /device:TPU:0, one launch (start us, length us, event | category | flops | bytes accessed | tf_op | source)
XLA Modules:
  0.0 494.3 jit_solution(15300777922348195923)
XLA Ops:
  6.5 0.0 copy-start
  6.5 0.0 all-gather.2.cloned.1.call-start
  6.5 0.7 all-gather.2.cloned.1.call-update
  7.3 0.0 reduce-scatter.2.cloned.1.call-start
  8.0 59.8 %all-gather.2.cloned.1.call-done = bf16[8192,256]{1,0:T(8,128)(2,1)} async-done(((bf16[512,256]{1,0:T(8,128)(2,1)}), bf16[8192,256]{1,0:T(8,128)(2,1)}) %all-gather.2.cloned.1.call-update) | async-done | bytes 4194320 | tf_op jit(solution)/shard_map/all_gather | solution.py:51
  67.8 2.5 broadcast_in_dim.23
  70.3 82.1 %while.14 = (s32[]{:T(128)}, f32[32,128,256]{2,1,0:T(8,128)}, f32[32,128]{1,0:T(8,128)S(1)}, s32[]{:T(128)}, s32[512]{0:T(512)}, /*index=5*/bf16[512,128,128]{2,...) while((s32[]{:T(128)}, f32[32,128,256]{2,1,0:T(8,128)}, ...), condition=%wide.region_4.5_spmd, body=%wide.region_0.4_spmd.sunk | while | flops 271587456 | bytes 25221328 | solution.py:41
  70.3 1.4 and_convert_fusion.2
  71.7 1.6 convert_reduce_fusion.2
  73.3 0.8 scatter_custom_fusion.8
  74.1 2.9 gather_fusion
  77.0 3.9 convolution_multiply_fusion.2
  80.9 9.9 %scatter_fusion = f32[32,128,256]{2,1,0:T(8,128)} fusion(f32[32,128,256]{2,1,0:T(8,128)} %get-tuple-element.210, s32[32]{0:T(128)S(1)} %get-tuple-element.193, f32[32,128,256]{2,1,0:T(8,128)} %convolution_multiply_fusion.2), kind=kCustom, calls=%fused_computation.1.clone.1 | custom fusion | flops 1048576 | bytes 12583040 | tf_op jit(solution)/shard_map/while/body/scatter-add | solution.py:35
  90.8 1.4 and_convert_fusion.2
  92.2 1.6 convert_reduce_fusion.2
  93.8 0.8 scatter_custom_fusion.8
  94.6 2.9 gather_fusion
  97.5 3.9 convolution_multiply_fusion.2
  101.4 9.9 %scatter_fusion = f32[32,128,256]{2,1,0:T(8,128)} fusion(f32[32,128,256]{2,1,0:T(8,128)} %get-tuple-element.210, s32[32]{0:T(128)S(1)} %get-tuple-element.193, f32[32,128,256]{2,1,0:T(8,128)} %convolution_multiply_fusion.2), kind=kCustom, calls=%fused_computation.1.clone.1 | custom fusion | flops 1048576 | bytes 12583040 | tf_op jit(solution)/shard_map/while/body/scatter-add | solution.py:35
  111.3 1.4 and_convert_fusion.2
  112.7 1.6 convert_reduce_fusion.2
  114.3 0.8 scatter_custom_fusion.8
  115.1 2.9 gather_fusion
  118.0 3.9 convolution_multiply_fusion.2
  121.9 10.0 %scatter_fusion = f32[32,128,256]{2,1,0:T(8,128)} fusion(f32[32,128,256]{2,1,0:T(8,128)} %get-tuple-element.210, s32[32]{0:T(128)S(1)} %get-tuple-element.193, f32[32,128,256]{2,1,0:T(8,128)} %convolution_multiply_fusion.2), kind=kCustom, calls=%fused_computation.1.clone.1 | custom fusion | flops 1048576 | bytes 12583040 | tf_op jit(solution)/shard_map/while/body/scatter-add | solution.py:35
  131.9 1.4 and_convert_fusion.2
  133.3 1.6 convert_reduce_fusion.2
  134.9 0.8 scatter_custom_fusion.8
  135.7 2.9 gather_fusion
  138.6 3.9 convolution_multiply_fusion.2
  142.5 9.9 %scatter_fusion = f32[32,128,256]{2,1,0:T(8,128)} fusion(f32[32,128,256]{2,1,0:T(8,128)} %get-tuple-element.210, s32[32]{0:T(128)S(1)} %get-tuple-element.193, f32[32,128,256]{2,1,0:T(8,128)} %convolution_multiply_fusion.2), kind=kCustom, calls=%fused_computation.1.clone.1 | custom fusion | flops 1048576 | bytes 12583040 | tf_op jit(solution)/shard_map/while/body/scatter-add | solution.py:35
  152.4 0.0 copy-start.3
  152.4 0.0 copy-start.1
  152.4 0.0 copy-start.2
  152.4 0.0 reduce-scatter.2.cloned.1.call-update
  152.4 0.6 copy-done.3
  153.0 0.6 dynamic-slice
  154.3 31.0 %all-reduce = f32[4096]{0:T(1024)S(1)} all-reduce(f32[4096]{0:T(1024)S(1)} %bitcast.15), channel_id=3, replica_groups=mesh['row'=16,'col'=8] {'col'}, use_global_device_ids=true, to_apply=%region_6.7.clone | all-reduce | flops 4096 | bytes 32768
  185.2 0.1 fusion.8
  185.3 300.1 %reduce-scatter.2.cloned.1.call-done = f32[512,256]{1,0:T(8,128)} async-done(((f32[4096,256]{1,0:T(8,128)}), f32[512,256]{1,0:T(8,128)}) %reduce-scatter.2.cloned.1.call-update) | async-done | bytes 524304 | tf_op jit(solution)/shard_map/reduce_scatter | solution.py:56
  485.4 0.0 copy-done
  485.4 0.0 copy-done.1
  485.4 0.0 copy-done.2
  485.4 2.0 fusion.6
  (9 shorter events, 0.1 us)
Async XLA Ops:
  6.5 478.9 %copy-start = (bf16[256,256]{1,0:T(8,128)(2,1)S(1)}, bf16[256,256]{1,0:T(8,128)(2,1)}, u32[]{:S(2)}) copy-start(bf16[256,256]{1,0:T(8,128)(2,1)} %param.12) | copy-start | bytes 393220
  6.5 61.3 %all-gather.2.cloned.1.call-start = ((), (), s32[]{:S(2)}) async-start(), calls=%async_computation.1 | async-start | bytes 4456448 | tf_op jit(solution)/shard_map/all_gather | solution.py:51
  7.3 478.1 %reduce-scatter.2.cloned.1.call-start = ((), (), s32[]{:S(2)}) async-start(), calls=%async_computation.2 | async-start | bytes 4718592 | tf_op jit(solution)/shard_map/reduce_scatter | solution.py:56
  152.4 0.7 copy-start.3
  152.4 333.0 %copy-start.1 = (bf16[512,256]{1,0:T(8,128)(2,1)S(1)}, bf16[512,256]{1,0:T(8,128)(2,1)}, u32[]{:S(2)}) copy-start(bf16[512,256]{1,0:T(8,128)(2,1)} %param.8) | copy-start | bytes 786436
  152.4 333.0 %copy-start.2 = (f32[256]{0:T(256)S(1)}, f32[256]{0:T(256)}, u32[]{:S(2)}) copy-start(f32[256]{0:T(256)} %param.13) | copy-start | bytes 3076
Sparse Core Ops, SparseCore 0:
  9.8 57.9 all-gather.1
  152.5 332.8 reduce-scatter.1
where the time goes:
time: 498 us; the launch traced here: 494 us
  waiting for transfers between devices  361 us (72%)
  other arithmetic  55 us (11%)
  blocking collectives  31 us (6%)
  matrix products  17.6 us (4%)
  local copies, waits for them, and re-layouts  15.2 us (3%)
  between operations  14.7 us (3%)
    reduce_scatter x1, waiting for transfers between devices, on_device(): lax.psum_scatter(part_total.reshape(-1, feature_width), 'col', scatter_di...  300 us
    all_gather x1, waiting for transfers between devices, on_device(): gathered = lax.all_gather(features, 'row', axis=0, tiled=True)  59.8 us
    scatter-add x4, other arithmetic, one_turn(): acc_total = acc_total.at[local_rows].add(products)  39.7 us
    unnamed x1, blocking collectives  31 us
    dot_general x4, matrix products, one_turn(): jnp.einsum('gij,gjf->gif', tile_block, sources, preferred_element_type=jn...  15.6 us
    gather x4, local copies, waits for them, and re-layouts, one_turn(): sources = sources_all[tile_cols]  11.5 us
  transfers between devices with their start and end apart: 2, of which 2 were waited for; matrix products, arithmetic and copies ran while one was open for 0% of the time, Pallas kernels for 0%

commit v1 on v0

v1 whole, which is shorter than its diff:
```python
import jax
import jax.numpy as jnp
from jax import lax
from jax.experimental import pallas as pl
from jax.experimental.pallas import tpu as pltpu
from jax.sharding import PartitionSpec as P

TILE = 128
F = 256
VP = 512
HALF = VP // 2
SLOTS = 512
PIECES = 16
OWNERS = 8
CHUNKS = 8
PER_CHUNK = SLOTS // CHUNKS
MESH = pl.DeviceIdType.MESH

N_GATHER = 19
N_REDUCE = 7


def kernel(
    count_ref, index_ref, features_ref, values_ref, weight_ref, bias_ref,
    out_ref,
    tiles, gathered, acc, sent, received, degree, degree_in, scale, inverse_v, inverse,
    load_sem, own_sem, inverse_sem, gs_sem, gr_sem, rs_sem, rr_sem, ds_sem, dr_sem,
):
    row = lax.axis_index("row")
    col = lax.axis_index("col")
    z, yh, core = row // 4, (row // 2) % 2, row % 2
    x, yl = col // 2, col % 2

    def in_row_group(dx, dy):
        xo = (x + dx) % 4
        yo = (yl + dy) % 2
        return {"row": row, "col": xo * 2 + yo}

    def in_col_group(dz, dy, dk):
        return {"row": ((z + dz) % 4) * 4 + ((yh + dy) % 2) * 2 + (core + dk) % 2, "col": col}

    def piece(dz, dy, dk=0):
        return ((z + dz) % 4) * 4 + ((yh + dy) % 2) * 2 + (core + dk) % 2

    loads = []
    for i in range(CHUNKS):
        part = pl.ds(i * PER_CHUNK, PER_CHUNK)
        loads.append(pltpu.make_async_copy(values_ref.at[part], tiles.at[part], load_sem.at[i]))
        loads[-1].start()
    own_copy = pltpu.make_async_copy(features_ref, gathered.at[row], own_sem)
    own_copy.start()

    others = [(dx, dy) for dx in range(4) for dy in range(2) if (dx, dy) != (0, 0)]
    barrier = pltpu.get_barrier_semaphore()
    near = [in_col_group(0, 0, 1), in_col_group(1, 0, 0), in_col_group(3, 0, 0), in_col_group(0, 1, 0)]
    far = [in_row_group(dx, dy) for dx, dy in others]
    for device in near + far:
        pl.semaphore_signal(barrier, inc=1, device_id=device, device_id_type=MESH)
    pl.semaphore_wait(barrier, len(near) + len(far))

    sends = []

    def remote(src, dst, send_sem, recv_sem, device):
        copy = pltpu.make_async_remote_copy(
            src_ref=src, dst_ref=dst, send_sem=send_sem, recv_sem=recv_sem,
            device_id=device, device_id_type=MESH,
        )
        copy.start()
        sends.append(copy)
        return copy

    def part_of(which, half):
        if half is None:
            return gathered.at[which]
        return gathered.at[which, pl.ds(half * HALF, HALF)]

    gather_count = [0]

    def gather_send(which, half, role, device, src=None):
        place = part_of(which, half)
        n = gather_count[0]
        gather_count[0] += 1
        remote(place if src is None else src, place, gs_sem.at[n], gr_sem.at[role], device)

    def gather_wait(which, half, role):
        place = part_of(which, half)
        pltpu.make_async_remote_copy(
            src_ref=place, dst_ref=place, send_sem=gs_sem.at[0], recv_sem=gr_sem.at[role],
            device_id=near[0], device_id_type=MESH,
        ).wait_recv()

    sibling, z_up, z_down, y_far = near

    gather_send(row, None, 1, z_up, features_ref)
    gather_send(row, None, 2, z_down, features_ref)
    gather_send(row, None, 3, y_far, features_ref)
    gather_send(row, None, 0, sibling, features_ref)

    live = count_ref[0]
    tiles[SLOTS] = jnp.zeros((TILE, TILE), jnp.bfloat16)
    place_id = (
        lax.broadcasted_iota(jnp.int32, (16, TILE), 0) * TILE
        + lax.broadcasted_iota(jnp.int32, (16, TILE), 1)
    )

    def mark(step, found):
        for u in range(16):
            slot = step * 16 + u
            position = jnp.where(slot < live, index_ref[slot], -1)
            found = jnp.where(place_id == position, slot, found)
        return found

    inverse_v[...] = lax.fori_loop(0, SLOTS // 16, mark, jnp.full((16, TILE), SLOTS, jnp.int32))
    inverse_copy = pltpu.make_async_copy(inverse_v, inverse, inverse_sem)
    inverse_copy.start()

    row_id = lax.broadcasted_iota(jnp.int32, (OWNERS * 8, TILE), 0)
    degree[...] = jnp.zeros_like(degree)
    for i in range(CHUNKS):
        loads[i].wait()
        marks, parts = [], []
        for u in range(PER_CHUNK):
            slot = i * PER_CHUNK + u
            tile_row = index_ref[slot] // 64
            at = jnp.where(slot < live, (tile_row // 4) * 8 + tile_row % 4, -1)
            marks.append((row_id == at).astype(jnp.float32).astype(jnp.bfloat16))
            parts.append(tiles[slot])
        sums = lax.dot_general(
            jnp.concatenate(marks, axis=1), jnp.concatenate(parts, axis=1),
            (((1,), (1,)), ((), ())), preferred_element_type=jnp.float32,
        )
        degree[...] += sums.reshape(degree.shape)

    for n, (dx, dy) in enumerate(others):
        target = ((x + dx) % 4) * 2 + (yl + dy) % 2
        remote(degree.at[target], degree_in.at[n], ds_sem.at[n], dr_sem.at[n], in_row_group(dx, dy))
    inverse_copy.wait()
    own_copy.wait()

    def block_of_a(first_row, rows, pieces):
        half_row = first_row // 2
        lines = []
        for a in range(rows):
            line = []
            for p in pieces:
                for b in range(4):
                    lane = (a % 2) * 64 + p * 4 + b
                    line.append(tiles[inverse[half_row + a // 2, lane]])
            lines.append(jnp.concatenate(line, axis=1))
        return jnp.concatenate(lines, axis=0)

    def product(first_row, rows, pieces):
        sources = jnp.concatenate([gathered[p] for p in pieces], axis=0)
        return jnp.dot(
            block_of_a(first_row, rows, pieces), sources, preferred_element_type=jnp.float32
        )

    def accumulate(pieces, first):
        def step(i, _):
            span = pl.ds(pl.multiple_of(i * 8 * TILE, 8 * TILE), 8 * TILE)
            value = product(i * 8, 8, pieces)
            acc[span, :] = value if first else acc[span, :] + value
            return 0

        lax.fori_loop(0, 4, step, 0)

    gather_wait(piece(0, 0, 1), None, 0)
    accumulate([piece(0, 0), piece(0, 0, 1)], True)

    gather_wait(piece(3, 0), None, 1)
    gather_send(piece(3, 0), 0, 4, z_up)
    gather_wait(piece(1, 0), None, 2)
    gather_send(piece(1, 0), 1, 5, z_down)
    gather_send(piece(3, 0), None, 10, sibling)
    gather_send(piece(1, 0), None, 11, sibling)
    gather_wait(piece(0, 1), None, 3)
    gather_send(piece(0, 1), None, 6, z_up)
    gather_send(piece(0, 1), None, 7, z_down)
    gather_send(piece(0, 1), None, 12, sibling)

    gather_wait(piece(3, 0, 1), None, 10)
    accumulate([piece(3, 0), piece(3, 0, 1)], False)

    gather_wait(piece(2, 0), 0, 4)
    gather_send(piece(2, 0), 0, 8, y_far)
    gather_wait(piece(2, 0), 1, 5)
    gather_send(piece(2, 0), 1, 9, y_far)
    gather_send(piece(2, 0), 0, 13, sibling)
    gather_send(piece(2, 0), 1, 14, sibling)

    gather_wait(piece(1, 0, 1), None, 11)
    accumulate([piece(1, 0), piece(1, 0, 1)], False)
    gather_wait(piece(0, 1, 1), None, 12)
    accumulate([piece(0, 1), piece(0, 1, 1)], False)

    gather_wait(piece(3, 1), None, 6)
    gather_send(piece(3, 1), None, 15, sibling)
    gather_wait(piece(1, 1), None, 7)
    gather_send(piece(1, 1), None, 16, sibling)
    gather_wait(piece(2, 1), 0, 8)
    gather_send(piece(2, 1), 0, 17, sibling)
    gather_wait(piece(2, 1), 1, 9)
    gather_send(piece(2, 1), 1, 18, sibling)

    gather_wait(piece(2, 0, 1), 0, 13)
    gather_wait(piece(2, 0, 1), 1, 14)
    gather_wait(piece(3, 1, 1), None, 15)
    gather_wait(piece(1, 1, 1), None, 16)
    gather_wait(piece(2, 1, 1), 0, 17)
    gather_wait(piece(2, 1, 1), 1, 18)

    last = [piece(2, 0), piece(2, 0, 1), piece(3, 1), piece(3, 1, 1),
            piece(1, 1), piece(1, 1, 1), piece(2, 1), piece(2, 1, 1)]

    x_up, x_down, y_near = in_row_group(1, 0), in_row_group(3, 0), in_row_group(0, 1)

    def finish(dx, dy):
        owner = ((x + dx) % 4) * 2 + (yl + dy) % 2
        span = pl.ds(pl.multiple_of(owner * VP, VP), VP)
        return acc[span, :] + product(owner * 4, 4, last)

    def reduce_send(role, value, device):
        sent[role] = value.astype(jnp.bfloat16)
        remote(sent.at[role], received.at[role], rs_sem.at[role], rr_sem.at[role], device)

    def reduce_wait(role):
        pltpu.make_async_remote_copy(
            src_ref=sent.at[role], dst_ref=received.at[role], send_sem=rs_sem.at[role],
            recv_sem=rr_sem.at[role], device_id=near[0], device_id_type=MESH,
        ).wait_recv()
        return received[role].astype(jnp.float32)

    reduce_send(0, finish(2, 1), x_up)
    reduce_send(1, finish(2, 0), x_down)
    reduce_send(3, finish(3, 1), x_down)
    reduce_send(4, finish(1, 0), x_up)
    partial = finish(1, 1)
    reduce_send(2, partial + reduce_wait(0), x_up)
    partial = finish(3, 0)
    reduce_send(5, partial + reduce_wait(1), x_down)
    span_f = pl.ds(pl.multiple_of((x * 2 + (yl + 1) % 2) * VP, VP), VP)
    span_m = pl.ds(pl.multiple_of(col * VP, VP), VP)
    acc[span_f, :] = finish(0, 1)
    acc[span_m, :] = finish(0, 0)

    total = degree[col]
    for n in range(len(others)):
        pltpu.make_async_remote_copy(
            src_ref=degree.at[0], dst_ref=degree_in.at[n], send_sem=ds_sem.at[n],
            recv_sem=dr_sem.at[n], device_id=near[0], device_id_type=MESH,
        ).wait_recv()
        total = total + degree_in[n]
    factor = lax.rsqrt(1.0 + total)
    diagonal = lax.broadcasted_iota(jnp.int32, (TILE, TILE), 0) == lax.broadcasted_iota(
        jnp.int32, (TILE, TILE), 1
    )
    for q in range(4):
        column = jnp.sum(jnp.where(diagonal, factor[q : q + 1, :], 0.0), axis=1, keepdims=True)
        scale[pl.ds(q * TILE, TILE), :] = jnp.broadcast_to(column, (TILE, TILE))

    reduce_send(6, acc[span_f, :] + reduce_wait(3) + reduce_wait(2), y_near)
    acc[span_m, :] += reduce_wait(4) + reduce_wait(5)
    last_part = reduce_wait(6)
    wide = jnp.concatenate([scale[...], scale[...]], axis=1)
    hidden = (acc[span_m, :] + last_part) * wide + gathered[row].astype(jnp.float32)
    mixed = jnp.dot(hidden.astype(jnp.bfloat16), weight_ref[...], preferred_element_type=jnp.float32)
    out_ref[...] = jnp.maximum(mixed + bias_ref[...], 0.0).astype(jnp.bfloat16)

    for copy in sends:
        copy.wait_send()


def on_device(features, tile_values, tile_index, tile_count, weight, out_bias):
    any_space = pl.BlockSpec(memory_space=pl.ANY)
    vmem = pl.BlockSpec(memory_space=pltpu.VMEM)
    smem = pl.BlockSpec(memory_space=pltpu.SMEM)
    dma = pltpu.SemaphoreType.DMA
    return pl.pallas_call(
        kernel,
        out_shape=jax.ShapeDtypeStruct((VP, F), jnp.bfloat16),
        in_specs=[smem, smem, any_space, any_space, vmem, vmem],
        out_specs=vmem,
        scratch_shapes=[
            pltpu.VMEM((SLOTS + 1, TILE, TILE), jnp.bfloat16),
            pltpu.VMEM((PIECES, VP, F), jnp.bfloat16),
            pltpu.VMEM((OWNERS * VP, F), jnp.float32),
            pltpu.VMEM((N_REDUCE, VP, F), jnp.bfloat16),
            pltpu.VMEM((N_REDUCE, VP, F), jnp.bfloat16),
            pltpu.VMEM((OWNERS, 8, TILE), jnp.float32),
            pltpu.VMEM((OWNERS - 1, 8, TILE), jnp.float32),
            pltpu.VMEM((VP, TILE), jnp.float32),
            pltpu.VMEM((16, TILE), jnp.int32),
            pltpu.SMEM((16, TILE), jnp.int32),
            dma((CHUNKS,)), dma, dma,
            dma((N_GATHER,)), dma((N_GATHER,)),
            dma((N_REDUCE,)), dma((N_REDUCE,)),
            dma((OWNERS - 1,)), dma((OWNERS - 1,)),
        ],
        compiler_params=pltpu.CompilerParams(
            collective_id=1, has_side_effects=True, vmem_limit_bytes=56 * 2**20
        ),
        name="graph_layer",
    )(
        tile_count.reshape(1),
        tile_index.reshape(SLOTS),
        features,
        tile_values.reshape(SLOTS, TILE, TILE),
        weight,
        out_bias.reshape(1, F),
    )


def solution(mesh):
    in_specs = (
        P(("row", "col"), None),
        P("row", "col", None, None, None),
        P("row", "col", None),
        P("row", "col"),
        P(),
        P(),
    )
    return jax.shard_map(
        on_device, mesh=mesh, in_specs=in_specs, out_specs=P(("row", "col"), None), check_vma=False
    )
```

time: 498 us -> 68.6 us (0.14)
  waiting for transfers between devices: 361 us -> 0 us
  Pallas kernels: 0 us -> 65.1 us
  other arithmetic: 55 us -> 0 us
  blocking collectives: 31 us -> 0 us
  matrix products: 17.6 us -> 0 us
  between operations: 14.7 us -> 0.66 us
  local copies, waits for them, and re-layouts: 15.2 us -> 1.67 us
    reduce_scatter x1 -> x0, waiting for transfers between devices: 300 us -> none  [on_device(): lax.psum_scatter(part_total.reshape(-1, feature_width), 'col', scatter_di...]
    pallas_call x0 -> x1, Pallas kernels: none -> 65.1 us  [on_device(): pl.pallas_call(kernel, out_shape=jax.ShapeDtypeStruct((VP, F), jnp.bfloat...]
    all_gather x1 -> x0, waiting for transfers between devices: 59.8 us -> none  [on_device(): gathered = lax.all_gather(features, 'row', axis=0, tiled=True)]
    scatter-add x8 -> x0, other arithmetic: 42.9 us -> none  [the longest x4 39.7 us: one_turn(): acc_total = acc_total.at[local_rows].add(products)]
    unnamed x1 -> x0, blocking collectives: 31 us -> none
    dot_general x5 -> x0, matrix products: 17.6 us -> none  [the longest x4 15.6 us: one_turn(): jnp.einsum('gij,gjf->gif', tile_block, sources, preferred_element_type=jn...]
    gather x4 -> x0, local copies, waits for them, and re-layouts: 11.5 us -> none  [one_turn(): sources = sources_all[tile_cols]]
    reduce_sum x4 -> x0, other arithmetic: 6.31 us -> none  [one_turn(): jnp.sum(tile_block, axis=2, dtype=jnp.float32) * live_mask[:, None]]
  transfers between devices with their start and end apart: 2 -> 0, of which waited for: 2 -> 0; matrix products, arithmetic and copies ran while one was open for 0% -> 0% of each run, Pallas kernels for 0% -> 0%
where the time goes in v1:
time: 68.6 us; the launch traced here: 67.5 us
  Pallas kernels  65.1 us (95%)
  local copies, waits for them, and re-layouts  1.67 us (2%)
    pallas_call x1, Pallas kernels, on_device(): pl.pallas_call(kernel, out_shape=jax.ShapeDtypeStruct((VP, F), jnp.bfloat...  65.1 us
    unnamed x1, local copies, waits for them, and re-layouts  1.67 us

profile of v1, /device:TPU:0, one launch (start us, length us, event | category | flops | bytes accessed | tf_op | source)
XLA Modules:
  0.0 67.5 jit_solution(12393823027426961735)
XLA Ops:
  0.7 65.1 %graph_layer.1 = bf16[512,256]{1,0:T(8,128)(2,1)} custom-call(s32[1]{0:T(128)} %bitcast.4.count_ref, s32[512]{0:T(512)} %bitcast.6, bf16[512,256]{1,0:T(8,128)(2,1)} %features_ref.1, bf16[512,128,128]{2,1,0:T(8,128)(2,1)} %bitcast.5, bf16[256,256]{1,0:T(8,128)(2,1)} %weight_ref.1, f32[1,256]{1,0:T(1,128)} %bitcast.7), custom_call_target="tpu_custom_call" | custom-call | tf_op jit(solution)/shard_map/graph_layer/pallas_call | solution.py:278
  65.8 1.7 %copy.9 = bf16[512,256]{1,0:T(8,128)(2,1)} copy(bf16[512,256]{1,0:T(8,128)(2,1)} %graph_layer.1) | data formatting | bytes 524288

commit v2 on v1

v2 whole, which is shorter than its diff:
```python
import jax
import jax.numpy as jnp
from jax import lax
from jax.experimental import pallas as pl
from jax.experimental.pallas import tpu as pltpu
from jax.sharding import PartitionSpec as P

TILE = 128
F = 256
VP = 512
HALF = VP // 2
SLOTS = 512
PIECES = 16
OWNERS = 8
CHUNKS = 8
PER_CHUNK = SLOTS // CHUNKS
MESH = pl.DeviceIdType.MESH

GATHER = (
    "own", "below_a", "below_b", "above_a", "above_b", "far_a", "far_b", "two_a", "two_b",
    "far_below_a", "far_below_b", "far_above_a", "far_above_b", "far_two_a", "far_two_b",
    "s_below", "s_above", "s_far", "s_two", "s_far_below", "s_far_above", "s_far_two",
)
REDUCE = (
    "f2_a", "f2_b", "f_up_a", "f_up_b", "f_down_a", "f_down_b", "relay_a", "relay_b",
    "m_up_a", "m_up_b", "m_down_a", "m_down_b", "f_a", "f_b",
)
N_GATHER, N_REDUCE = len(GATHER), len(REDUCE)
EARLY = 4


def kernel(
    count_ref, index_ref, features_ref, values_ref, weight_ref, bias_ref,
    out_ref,
    tiles, gathered, acc, sent, received, degree, degree_in, scale, inverse_v, inverse,
    load_sem, own_sem, inverse_sem, gs_sem, gr_sem, rs_sem, rr_sem, ds_sem, dr_sem,
):
    row = lax.axis_index("row")
    col = lax.axis_index("col")
    z, yh, core = row // 4, (row // 2) % 2, row % 2
    x, yl = col // 2, col % 2

    def owner(dx, dy):
        return ((x + dx) % 4) * 2 + (yl + dy) % 2

    def piece(dz, dy, dk=0):
        return ((z + dz) % 4) * 4 + ((yh + dy) % 2) * 2 + (core + dk) % 2

    def in_row_group(dx, dy):
        return {"row": row, "col": owner(dx, dy)}

    def in_col_group(dz, dy, dk):
        return {"row": piece(dz, dy, dk), "col": col}

    def load(i):
        part = pl.ds(i * PER_CHUNK, PER_CHUNK)
        return pltpu.make_async_copy(values_ref.at[part], tiles.at[part], load_sem.at[i])

    sibling, z_up, z_down, y_far = (
        in_col_group(0, 0, 1), in_col_group(1, 0, 0), in_col_group(3, 0, 0), in_col_group(0, 1, 0)
    )
    x_up, x_down, y_near = in_row_group(1, 0), in_row_group(3, 0), in_row_group(0, 1)
    others = [(dx, dy) for dx in range(4) for dy in range(2) if (dx, dy) != (0, 0)]
    near = [sibling, z_up, z_down, y_far]
    far = [in_row_group(dx, dy) for dx, dy in others]

    barrier = pltpu.get_barrier_semaphore()
    for device in near + far:
        pl.semaphore_signal(barrier, inc=1, device_id=device, device_id_type=MESH)
    for i in range(CHUNKS):
        load(i).start()
    own_copy = pltpu.make_async_copy(features_ref, gathered.at[row], own_sem)
    own_copy.start()

    live = count_ref[0]
    tiles[SLOTS] = jnp.zeros((TILE, TILE), jnp.bfloat16)
    place_id = (
        lax.broadcasted_iota(jnp.int32, (16, TILE), 0) * TILE
        + lax.broadcasted_iota(jnp.int32, (16, TILE), 1)
    )

    def mark(step, found):
        for u in range(16):
            slot = step * 16 + u
            position = jnp.where(slot < live, index_ref[slot], -1)
            found = jnp.where(place_id == position, slot, found)
        return found

    inverse_v[...] = lax.fori_loop(0, SLOTS // 16, mark, jnp.full((16, TILE), SLOTS, jnp.int32))
    inverse_copy = pltpu.make_async_copy(inverse_v, inverse, inverse_sem)
    inverse_copy.start()
    pl.semaphore_wait(barrier, len(near) + len(far))

    halves = {"a": pl.ds(0, HALF), "b": pl.ds(HALF, HALF)}

    def view(which, half):
        return gathered.at[which] if half is None else gathered.at[which, halves[half]]

    gather_sends = []

    def gather_copy(which, half, role, device, own):
        place = view(which, half)
        source = place
        if own:
            source = features_ref if half is None else features_ref.at[halves[half]]
        n = GATHER.index(role)
        return pltpu.make_async_remote_copy(
            src_ref=source, dst_ref=place, send_sem=gs_sem.at[n], recv_sem=gr_sem.at[n],
            device_id=device, device_id_type=MESH,
        )

    def gather_send(which, half, role, device, own=False):
        gather_copy(which, half, role, device, own).start()
        gather_sends.append((half, role))

    def gather_wait(which, half, role):
        gather_copy(which, half, role, sibling, False).wait_recv()

    gather_send(row, "a", "below_a", z_up, True)
    gather_send(row, "b", "above_b", z_down, True)
    gather_send(row, "a", "far_a", y_far, True)
    gather_send(row, "b", "far_b", y_far, True)
    gather_send(row, "b", "below_b", z_up, True)
    gather_send(row, "a", "above_a", z_down, True)
    gather_send(row, None, "own", sibling, True)

    def forward_neighbours():
        gather_wait(piece(3, 0), "a", "below_a")
        gather_send(piece(3, 0), "a", "two_a", z_up)
        gather_wait(piece(1, 0), "b", "above_b")
        gather_send(piece(1, 0), "b", "two_b", z_down)

    def forward_far():
        gather_wait(piece(0, 1), "a", "far_a")
        gather_send(piece(0, 1), "a", "far_below_a", z_up)
        gather_wait(piece(0, 1), "b", "far_b")
        gather_send(piece(0, 1), "b", "far_above_b", z_down)
        gather_wait(piece(3, 0), "b", "below_b")
        gather_send(piece(3, 0), None, "s_below", sibling)
        gather_wait(piece(1, 0), "a", "above_a")
        gather_send(piece(1, 0), None, "s_above", sibling)
        gather_send(piece(0, 1), "b", "far_below_b", z_up)
        gather_send(piece(0, 1), "a", "far_above_a", z_down)
        gather_send(piece(0, 1), None, "s_far", sibling)

    def forward_two():
        gather_wait(piece(2, 0), "a", "two_a")
        gather_send(piece(2, 0), "a", "far_two_a", y_far)
        gather_wait(piece(2, 0), "b", "two_b")
        gather_send(piece(2, 0), "b", "far_two_b", y_far)
        gather_send(piece(2, 0), None, "s_two", sibling)

    def forward_far_below():
        gather_wait(piece(3, 1), "a", "far_below_a")
        gather_wait(piece(3, 1), "b", "far_below_b")
        gather_send(piece(3, 1), None, "s_far_below", sibling)

    def forward_far_above():
        gather_wait(piece(1, 1), "a", "far_above_a")
        gather_wait(piece(1, 1), "b", "far_above_b")
        gather_send(piece(1, 1), None, "s_far_above", sibling)

    def forward_far_two():
        gather_wait(piece(2, 1), "a", "far_two_a")
        gather_wait(piece(2, 1), "b", "far_two_b")
        gather_send(piece(2, 1), None, "s_far_two", sibling)

    row_id = lax.broadcasted_iota(jnp.int32, (OWNERS * 8, TILE), 0)
    degree[...] = jnp.zeros_like(degree)

    def add_degrees(i, _):
        marks, parts = [], []
        for u in range(PER_CHUNK):
            slot = i * PER_CHUNK + u
            tile_row = index_ref[slot] // 64
            at = jnp.where(slot < live, (tile_row // 4) * 8 + tile_row % 4, -1)
            marks.append((row_id == at).astype(jnp.float32).astype(jnp.bfloat16))
            parts.append(tiles[slot])
        sums = lax.dot_general(
            jnp.concatenate(marks, axis=1), jnp.concatenate(parts, axis=1),
            (((1,), (1,)), ((), ())), preferred_element_type=jnp.float32,
        )
        degree[...] += sums.reshape(degree.shape)
        return 0

    def load_and_add(i, _):
        load(i).wait()
        return add_degrees(i, 0)

    acc[...] = jnp.zeros_like(acc)
    lax.fori_loop(0, EARLY, load_and_add, 0)
    for i in range(EARLY, CHUNKS):
        load(i).wait()
    inverse_copy.wait()
    own_copy.wait()

    def product(first_row, rows, pieces):
        half_row = first_row // 2
        lines = []
        for a in range(rows):
            line = []
            for p in pieces:
                for b in range(4):
                    lane = (a % 2) * 64 + p * 4 + b
                    line.append(tiles[inverse[half_row + a // 2, lane]])
            lines.append(jnp.concatenate(line, axis=1))
        sources = jnp.concatenate([gathered[p] for p in pieces], axis=0)
        return jnp.dot(
            jnp.concatenate(lines, axis=0), sources, preferred_element_type=jnp.float32
        )

    def multiply(step, _):
        pair, part = step // 4, step % 4
        dz, dy = ((pair * 3) % 5) % 4, pair // 3
        for at, action in PLAN:
            pl.when(step == at)(action)
        span = pl.ds(pl.multiple_of(part * 8 * TILE, 8 * TILE), 8 * TILE)
        acc[span, :] += product(part * 8, 8, [piece(dz, dy), piece(dz, dy, 1)])
        return 0

    def need(which, role):
        return lambda: gather_wait(piece(*which), None, role)

    def late_degrees():
        lax.fori_loop(EARLY, CHUNKS, add_degrees, 0)

    PLAN = [
        (0, need((0, 0, 1), "own")),
        (2, forward_neighbours),
        (4, forward_far),
        (4, late_degrees),
        (4, need((3, 0, 1), "s_below")),
        (6, forward_two),
        (8, need((1, 0, 1), "s_above")),
        (11, forward_far_below),
        (12, need((0, 1, 1), "s_far")),
        (12, forward_far_above),
        (14, forward_far_two),
    ]
    lax.fori_loop(0, 16, multiply, 0)
    for which, role in (
        ((2, 0, 1), "s_two"), ((3, 1, 1), "s_far_below"), ((1, 1, 1), "s_far_above"),
        ((2, 1, 1), "s_far_two"),
    ):
        gather_wait(piece(*which), None, role)

    last = [piece(dz, dy, dk) for dz, dy in ((2, 0), (3, 1), (1, 1), (2, 1)) for dk in (0, 1)]

    def rows_of(dx, dy, half):
        start = owner(dx, dy) * VP + (HALF if half == "b" else 0)
        return pl.ds(pl.multiple_of(start, HALF), HALF)

    def part(dx, dy, half):
        return acc[rows_of(dx, dy, half), :]

    def reduce_copy(role, device):
        n = REDUCE.index(role)
        return pltpu.make_async_remote_copy(
            src_ref=sent.at[n], dst_ref=received.at[n], send_sem=rs_sem.at[n], recv_sem=rr_sem.at[n],
            device_id=device, device_id_type=MESH,
        )

    def reduce_send(role, value, device):
        sent[REDUCE.index(role)] = value.astype(jnp.bfloat16)
        reduce_copy(role, device).start()

    def reduced(role):
        reduce_copy(role, sibling).wait_recv()
        return received[REDUCE.index(role)].astype(jnp.float32)

    def after_0():
        reduce_send("f2_a", part(2, 1, "a"), y_near)
        reduce_send("f2_b", part(2, 1, "b"), y_near)

    def after_1():
        reduce_send("f_up_a", part(1, 1, "a"), x_up)
        reduce_send("f_up_b", part(1, 1, "b"), x_up)

    def after_2():
        reduce_send("f_down_a", part(3, 1, "a"), x_down)
        reduce_send("f_down_b", part(3, 1, "b"), x_down)

    def after_4():
        reduce_send("m_up_b", part(1, 0, "b"), x_up)
        reduce_send("relay_a", part(2, 0, "a") + reduced("f2_a"), x_up)
        reduce_send("relay_b", part(2, 0, "b") + reduced("f2_b"), x_down)

    def after_5():
        reduce_send("m_down_a", part(3, 0, "a"), x_down)

    def after_6():
        reduce_send("f_a", part(0, 1, "a") + reduced("f_up_a") + reduced("f_down_a"), y_near)
        reduce_send("f_b", part(0, 1, "b") + reduced("f_up_b") + reduced("f_down_b"), y_near)

    def after_7():
        reduce_send("m_up_a", part(1, 0, "a") + reduced("relay_a"), x_up)
        reduce_send("m_down_b", part(3, 0, "b") + reduced("relay_b"), x_down)

    def finish(i, _):
        turn = i % 3
        dx = jnp.where(i >= 6, 0, jnp.where(turn == 0, 2, jnp.where(turn == 1, 1, 3)))
        dy = jnp.where((i < 3) | (i == 6), 1, 0)
        to = owner(dx, dy)
        span = pl.ds(pl.multiple_of(to * VP, VP), VP)
        acc[span, :] += product(to * 4, 4, last)
        for at, action in (
            (0, after_0), (1, after_1), (2, after_2), (4, after_4), (5, after_5), (6, after_6),
            (7, after_7),
        ):
            pl.when(i == at)(action)
        return 0

    def degree_copy(n, dx, dy):
        return pltpu.make_async_remote_copy(
            src_ref=degree.at[owner(dx, dy)], dst_ref=degree_in.at[n], send_sem=ds_sem.at[n],
            recv_sem=dr_sem.at[n], device_id=far[n], device_id_type=MESH,
        )

    for n, (dx, dy) in enumerate(others):
        degree_copy(n, dx, dy).start()
    lax.fori_loop(0, 8, finish, 0)

    total = degree[col]
    for n, (dx, dy) in enumerate(others):
        degree_copy(n, dx, dy).wait_recv()
        total = total + degree_in[n]
    factor = lax.rsqrt(1.0 + total)
    diagonal = lax.broadcasted_iota(jnp.int32, (TILE, TILE), 0) == lax.broadcasted_iota(
        jnp.int32, (TILE, TILE), 1
    )
    for q in range(4):
        column = jnp.sum(jnp.where(diagonal, factor[q : q + 1, :], 0.0), axis=1, keepdims=True)
        scale[pl.ds(q * TILE, TILE), :] = jnp.broadcast_to(column, (TILE, TILE))

    for half in "ab":
        aggregate = part(0, 0, half) + reduced("m_down_" + half) + reduced("m_up_" + half)
        aggregate = aggregate + reduced("f_" + half)
        here = halves[half]
        wide = jnp.concatenate([scale[here, :], scale[here, :]], axis=1)
        hidden = aggregate * wide + gathered[row, here].astype(jnp.float32)
        mixed = jnp.dot(
            hidden.astype(jnp.bfloat16), weight_ref[...], preferred_element_type=jnp.float32
        )
        out_ref[here, :] = jnp.maximum(mixed + bias_ref[...], 0.0).astype(jnp.bfloat16)

    for half, role in gather_sends:
        gather_copy(0, half, role, sibling, False).wait_send()
    for role in REDUCE:
        reduce_copy(role, sibling).wait_send()
    for n, (dx, dy) in enumerate(others):
        degree_copy(n, dx, dy).wait_send()


def on_device(features, tile_values, tile_index, tile_count, weight, out_bias):
    any_space = pl.BlockSpec(memory_space=pl.ANY)
    vmem = pl.BlockSpec(memory_space=pltpu.VMEM)
    smem = pl.BlockSpec(memory_space=pltpu.SMEM)
    dma = pltpu.SemaphoreType.DMA
    return pl.pallas_call(
        kernel,
        out_shape=pltpu.VMEM((VP, F), jnp.bfloat16),
        in_specs=[smem, smem, any_space, any_space, vmem, vmem],
        out_specs=vmem,
        scratch_shapes=[
            pltpu.VMEM((SLOTS + 1, TILE, TILE), jnp.bfloat16),
            pltpu.VMEM((PIECES, VP, F), jnp.bfloat16),
            pltpu.VMEM((OWNERS * VP, F), jnp.float32),
            pltpu.VMEM((N_REDUCE, HALF, F), jnp.bfloat16),
            pltpu.VMEM((N_REDUCE, HALF, F), jnp.bfloat16),
            pltpu.VMEM((OWNERS, 8, TILE), jnp.float32),
            pltpu.VMEM((OWNERS - 1, 8, TILE), jnp.float32),
            pltpu.VMEM((VP, TILE), jnp.float32),
            pltpu.VMEM((16, TILE), jnp.int32),
            pltpu.SMEM((16, TILE), jnp.int32),
            dma((CHUNKS,)), dma, dma,
            dma((N_GATHER,)), dma((N_GATHER,)),
            dma((N_REDUCE,)), dma((N_REDUCE,)),
            dma((OWNERS - 1,)), dma((OWNERS - 1,)),
        ],
        compiler_params=pltpu.CompilerParams(
            collective_id=1, has_side_effects=True, vmem_limit_bytes=56 * 2**20
        ),
        name="graph_layer",
    )(
        tile_count.reshape(1),
        tile_index.reshape(SLOTS),
        features,
        tile_values.reshape(SLOTS, TILE, TILE),
        weight,
        out_bias.reshape(1, F),
    )


def solution(mesh):
    in_specs = (
        P(("row", "col"), None),
        P("row", "col", None, None, None),
        P("row", "col", None),
        P("row", "col"),
        P(),
        P(),
    )
    return jax.shard_map(
        on_device, mesh=mesh, in_specs=in_specs, out_specs=P(("row", "col"), None), check_vma=False
    )
```

time: 68.6 us -> 53.3 us (0.78); the launches traced: 67.5 us -> 53.2 us
  Pallas kernels: 65.1 us -> 51.8 us
  local copies, waits for them, and re-layouts: 1.67 us -> 0.71 us
    pallas_call x1, Pallas kernels: 65.1 us -> 51.8 us  [on_device(): pl.pallas_call(kernel, out_shape=pltpu.VMEM((VP, F), jnp.bfloat16), in_sp...]
    unnamed x1, local copies, waits for them, and re-layouts: 1.67 us -> 0.71 us
where the time goes in v2:
time: 53.3 us; the launch traced here: 53.2 us
  Pallas kernels  51.8 us (97%)
  local copies, waits for them, and re-layouts  0.71 us (1%)
  between operations  0.66 us (1%)
    pallas_call x1, Pallas kernels, on_device(): pl.pallas_call(kernel, out_shape=pltpu.VMEM((VP, F), jnp.bfloat16), in_sp...  51.8 us

profile of v2, /device:TPU:0, one launch (start us, length us, event | category | flops | bytes accessed | tf_op | source)
XLA Modules:
  0.0 53.2 jit_solution(6242757535638585694)
XLA Ops:
  0.7 51.8 %graph_layer.1 = bf16[512,256]{1,0:T(8,128)(2,1)S(1)} custom-call(s32[1]{0:T(128)} %bitcast.4.count_ref, s32[512]{0:T(512)} %bitcast.6, bf16[512,256]{1,0:T(8,128)(2,1)} %features_ref.1, bf16[512,128,128]{2,1,0:T(8,128)(2,1)} %bitcast.5, bf16[256,256]{1,0:T(8,128)(2,1)} %weight_ref.1, f32[1,256]{1,0:T(1,128)} %bitcast.7), custom_call_target="tpu_custom_call" | custom-call | tf_op jit(solution)/shard_map/graph_layer/pallas_call | solution.py:359
  52.5 0.7 %copy.8 = bf16[512,256]{1,0:T(8,128)(2,1)} copy(bf16[512,256]{1,0:T(8,128)(2,1)S(1)} %graph_layer.1) | data formatting | bytes 524288

commit v3 on v2

--- a/solution.py
+++ b/solution.py
@@ -26,7 +26,7 @@
     "m_up_a", "m_up_b", "m_down_a", "m_down_b", "f_a", "f_b",
 )
 N_GATHER, N_REDUCE = len(GATHER), len(REDUCE)
-EARLY = 4
+EARLY = 5
 
 
 def kernel(
@@ -226,16 +226,16 @@
 
     PLAN = [
         (0, need((0, 0, 1), "own")),
-        (2, forward_neighbours),
+        (1, forward_neighbours),
         (4, forward_far),
         (4, late_degrees),
+        (4, forward_two),
         (4, need((3, 0, 1), "s_below")),
-        (6, forward_two),
         (8, need((1, 0, 1), "s_above")),
-        (11, forward_far_below),
+        (10, forward_far_below),
+        (11, forward_far_above),
         (12, need((0, 1, 1), "s_far")),
-        (12, forward_far_above),
-        (14, forward_far_two),
+        (13, forward_far_two),
     ]
     lax.fori_loop(0, 16, multiply, 0)
     for which, role in (
@@ -270,42 +270,43 @@
 
     def after_0():
         reduce_send("f2_a", part(2, 1, "a"), y_near)
+
+    def after_1():
         reduce_send("f2_b", part(2, 1, "b"), y_near)
-
-    def after_1():
         reduce_send("f_up_a", part(1, 1, "a"), x_up)
+
+    def after_2():
         reduce_send("f_up_b", part(1, 1, "b"), x_up)
-
-    def after_2():
         reduce_send("f_down_a", part(3, 1, "a"), x_down)
-        reduce_send("f_down_b", part(3, 1, "b"), x_down)
+
+    def after_3():
+        reduce_send("f_down_b", part(3, 1, "b"), y_near)
+        reduce_send("relay_a", part(2, 0, "a") + reduced("f2_a"), x_up)
 
     def after_4():
+        reduce_send("relay_b", part(2, 0, "b") + reduced("f2_b"), x_down)
+
+    def after_5():
+        reduce_send("f_a", part(0, 1, "a") + reduced("f_up_a") + reduced("f_down_a"), y_near)
         reduce_send("m_up_b", part(1, 0, "b"), x_up)
-        reduce_send("relay_a", part(2, 0, "a") + reduced("f2_a"), x_up)
-        reduce_send("relay_b", part(2, 0, "b") + reduced("f2_b"), x_down)
-
-    def after_5():
+
+    def after_6():
+        reduce_send("f_b", part(0, 1, "b") + reduced("f_up_b"), y_near)
         reduce_send("m_down_a", part(3, 0, "a"), x_down)
-
-    def after_6():
-        reduce_send("f_a", part(0, 1, "a") + reduced("f_up_a") + reduced("f_down_a"), y_near)
-        reduce_send("f_b", part(0, 1, "b") + reduced("f_up_b") + reduced("f_down_b"), y_near)
 
     def after_7():
         reduce_send("m_up_a", part(1, 0, "a") + reduced("relay_a"), x_up)
-        reduce_send("m_down_b", part(3, 0, "b") + reduced("relay_b"), x_down)
+        reduce_send("m_down_b", part(3, 0, "b") + reduced("relay_b") + reduced("f_down_b"), x_down)
 
     def finish(i, _):
-        turn = i % 3
-        dx = jnp.where(i >= 6, 0, jnp.where(turn == 0, 2, jnp.where(turn == 1, 1, 3)))
-        dy = jnp.where((i < 3) | (i == 6), 1, 0)
+        dx = jnp.where((i == 0) | (i == 3), 2, jnp.where((i == 1) | (i == 5), 1, jnp.where((i == 2) | (i == 6), 3, 0)))
+        dy = jnp.where((i < 3) | (i == 4), 1, 0)
         to = owner(dx, dy)
         span = pl.ds(pl.multiple_of(to * VP, VP), VP)
         acc[span, :] += product(to * 4, 4, last)
         for at, action in (
-            (0, after_0), (1, after_1), (2, after_2), (4, after_4), (5, after_5), (6, after_6),
-            (7, after_7),
+            (0, after_0), (1, after_1), (2, after_2), (3, after_3), (4, after_4), (5, after_5),
+            (6, after_6), (7, after_7),
         ):
             pl.when(i == at)(action)
         return 0

time: 53.3 us -> 50.4 us (0.946)
  Pallas kernels: 51.8 us -> 48.9 us
    pallas_call x1, Pallas kernels: 51.8 us -> 48.9 us  [on_device(): pl.pallas_call(kernel, out_shape=pltpu.VMEM((VP, F), jnp.bfloat16), in_sp...]
where the time goes in v3:
time: 50.4 us; the launch traced here: 50.3 us
  Pallas kernels  48.9 us (97%)
  local copies, waits for them, and re-layouts  0.71 us (1%)
  between operations  0.66 us (1%)
    pallas_call x1, Pallas kernels, on_device(): pl.pallas_call(kernel, out_shape=pltpu.VMEM((VP, F), jnp.bfloat16), in_sp...  48.9 us

profile of v3, /device:TPU:0, one launch (start us, length us, event | category | flops | bytes accessed | tf_op | source)
XLA Modules:
  0.0 50.3 jit_solution(12952842036462726876)
XLA Ops:
  0.7 48.9 %graph_layer.1 = bf16[512,256]{1,0:T(8,128)(2,1)S(1)} custom-call(s32[1]{0:T(128)} %bitcast.4.count_ref, s32[512]{0:T(512)} %bitcast.6, bf16[512,256]{1,0:T(8,128)(2,1)} %features_ref.1, bf16[512,128,128]{2,1,0:T(8,128)(2,1)} %bitcast.5, bf16[256,256]{1,0:T(8,128)(2,1)} %weight_ref.1, f32[1,256]{1,0:T(1,128)} %bitcast.7), custom_call_target="tpu_custom_call" | custom-call | tf_op jit(solution)/shard_map/graph_layer/pallas_call | solution.py:360
  49.6 0.7 %copy.8 = bf16[512,256]{1,0:T(8,128)(2,1)} copy(bf16[512,256]{1,0:T(8,128)(2,1)S(1)} %graph_layer.1) | data formatting | bytes 524288

commit v4 on v3

--- a/solution.py
+++ b/solution.py
@@ -209,14 +209,17 @@
             jnp.concatenate(lines, axis=0), sources, preferred_element_type=jnp.float32
         )
 
-    def multiply(step, _):
-        pair, part = step // 4, step % 4
-        dz, dy = ((pair * 3) % 5) % 4, pair // 3
-        for at, action in PLAN:
-            pl.when(step == at)(action)
-        span = pl.ds(pl.multiple_of(part * 8 * TILE, 8 * TILE), 8 * TILE)
-        acc[span, :] += product(part * 8, 8, [piece(dz, dy), piece(dz, dy, 1)])
-        return 0
+    def multiply(pairs, plan):
+        pieces = [piece(dz, dy, dk) for dz, dy in pairs for dk in (0, 1)]
+
+        def step(part, _):
+            for at, action in plan:
+                pl.when(part == at)(action)
+            span = pl.ds(pl.multiple_of(part * 8 * TILE, 8 * TILE), 8 * TILE)
+            acc[span, :] += product(part * 8, 8, pieces)
+            return 0
+
+        lax.fori_loop(0, 4, step, 0)
 
     def need(which, role):
         return lambda: gather_wait(piece(*which), None, role)
@@ -224,20 +227,25 @@
     def late_degrees():
         lax.fori_loop(EARLY, CHUNKS, add_degrees, 0)
 
-    PLAN = [
+    multiply([(0, 0)], [
         (0, need((0, 0, 1), "own")),
         (1, forward_neighbours),
-        (4, forward_far),
-        (4, late_degrees),
-        (4, forward_two),
-        (4, need((3, 0, 1), "s_below")),
-        (8, need((1, 0, 1), "s_above")),
-        (10, forward_far_below),
-        (11, forward_far_above),
-        (12, need((0, 1, 1), "s_far")),
-        (13, forward_far_two),
-    ]
-    lax.fori_loop(0, 16, multiply, 0)
+    ])
+    multiply([(3, 0)], [
+        (0, forward_far),
+        (0, late_degrees),
+        (0, need((3, 0, 1), "s_below")),
+        (0, forward_two),
+    ])
+    multiply([(1, 0)], [
+        (0, need((1, 0, 1), "s_above")),
+        (2, forward_far_below),
+        (3, forward_far_above),
+    ])
+    multiply([(0, 1)], [
+        (0, need((0, 1, 1), "s_far")),
+        (1, forward_far_two),
+    ])
     for which, role in (
         ((2, 0, 1), "s_two"), ((3, 1, 1), "s_far_below"), ((1, 1, 1), "s_far_above"),
         ((2, 1, 1), "s_far_two"),

time: 50.4 us -> 50.1 us (level)
  no operation moved by 1% of the time
where the time goes in v4:
time: 50.1 us; the launch traced here: 50 us
  Pallas kernels  48.6 us (97%)
  local copies, waits for them, and re-layouts  0.71 us (1%)
  between operations  0.66 us (1%)
    pallas_call x1, Pallas kernels, on_device(): pl.pallas_call(kernel, out_shape=pltpu.VMEM((VP, F), jnp.bfloat16), in_sp...  48.6 us

profile of v4, /device:TPU:0, one launch (start us, length us, event | category | flops | bytes accessed | tf_op | source)
XLA Modules:
  0.0 50.0 jit_solution(16626450948499442726)
XLA Ops:
  0.7 48.6 %graph_layer.1 = bf16[512,256]{1,0:T(8,128)(2,1)S(1)} custom-call(s32[1]{0:T(128)} %bitcast.4.count_ref, s32[512]{0:T(512)} %bitcast.6, bf16[512,256]{1,0:T(8,128)(2,1)} %features_ref.1, bf16[512,128,128]{2,1,0:T(8,128)(2,1)} %bitcast.5, bf16[256,256]{1,0:T(8,128)(2,1)} %weight_ref.1, f32[1,256]{1,0:T(1,128)} %bitcast.7), custom_call_target="tpu_custom_call" | custom-call | tf_op jit(solution)/shard_map/graph_layer/pallas_call | solution.py:368
  49.3 0.7 %copy.8 = bf16[512,256]{1,0:T(8,128)(2,1)} copy(bf16[512,256]{1,0:T(8,128)(2,1)S(1)} %graph_layer.1) | data formatting | bytes 524288
